TPU v7x, 32 devices: a whole 2x2x4 slice. The times are simulated.
32 devices in a mesh: lon: 4 (over y, x), lat: 8 (over z, core).
Axes of the slice: x: 2, y: 2, z: 4, core: 2. Of those that a mesh axis runs over, the one named last changes fastest.
Arguments:
- adjoint: float32 [4, 10, 512, 2048], P(None, None, 'lat', 'lon'), may hold values from -6 to 6
- trajectory: float32 [4, 10, 512, 2048], P(None, None, 'lat', 'lon'), may hold values from -6 to 6
- diffusivity: float32 [10, 512, 2048], P(None, 'lat', 'lon'), may hold values from 0.06 to 0.24
- land_mask: int32 [10, 512, 2048], P(None, 'lat', 'lon'), may hold values 0 or 1
- coriolis: float32 [512], P('lat'), may hold values from -0.3 to 0.3
- obs_values: float32 [4096, 128], P(('lon', 'lat')), may hold values from -6 to 6
- obs_weight: float32 [4096], P(('lon', 'lat')), may hold values from 0.5 to 4
- obs_owner: int32 [4096, 1], P(('lon', 'lat')), may hold values from 0 to 31; in each aligned block of 128 rows (0 to 127, 128 to 255, ...) at most 8 rows name the same one
- obs_offset: int32 [4096], P(('lon', 'lat')), may hold values from 0 to 10239
- fold_partner: int32 [2048], P('lon'), may hold values from 0 to 2047, as said below
Outputs:
- adjoint_out: float32 [4, 10, 512, 2048], P(None, None, 'lat', 'lon')
Inputs may be any that keep to these rules, and one draw needn't show every extreme that they name: `obs_owner`: in the rows of one device no owner is named by more than 8 rows, a bound that some block reaches. fold_partner is the mirror of the tripolar fold: fold_partner[i] = (2047 - i + o) modulo 2048 for one even offset o.
All inputs are finite; a program needn't handle non-finite values. No bound on the sum of `land_mask` on one device may be relied on, other than what follows from the above.
Results may differ from a plain program's by a relative error of at most 0.000059.
Values sent between devices are 32-bit elements; how exact they have to be, the bound alone decides.
A program may use at most 320 MiB of HBM per device.

v0:
```python
import jax
import jax.numpy as jnp
from jax import lax
from jax.sharding import PartitionSpec as P

NSUB = 3
CAP = 8


def padded_2(shard, sides, width, wrap):
    for axis, dim in sides:
        count, length = (lax.axis_size(axis), shard.shape[dim])
        up = [(i, (i + 1) % count) for i in range(count if wrap else count - 1)]
        down = [(j, i) for i, j in up]
        last = lax.slice_in_dim(shard, length - width, length, axis=dim)
        initial = lax.slice_in_dim(shard, 0, width, axis=dim)
        before = lax.ppermute(last, axis, up)
        after = lax.ppermute(initial, axis, down)
        shard = jnp.concatenate([before, shard, after], axis=dim)
    return shard


def rim_cells(field_block, field_sign, fold_partner, rim_width):
    rows_here = field_block.shape[2]
    top_rows = field_block[:, :, rows_here - rim_width :, :]
    whole_top = lax.all_gather(top_rows, "lon", axis=3, tiled=True)
    ghost_rows = field_sign * jnp.take(whole_top[:, :, ::-1, :], fold_partner, axis=3)
    padded = padded_2(field_block, (("lat", 2),), rim_width, False)
    is_top = lax.axis_index("lat") == lax.axis_size("lat") - 1
    upper_rows = jnp.where(is_top, ghost_rows, padded[:, :, rows_here + rim_width :, :])
    padded = jnp.concatenate([padded[:, :, : rows_here + rim_width, :], upper_rows], axis=2)
    return padded_2(padded, (("lon", 3),), rim_width, True)


def mix_step(extended, coeffs):
    centre = extended[:, :, 1:-1, 1:-1]
    laplace = (
        extended[:, :, 1:-1, 2:]
        + extended[:, :, 1:-1, :-2]
        + extended[:, :, 2:, 1:-1]
        + extended[:, :, :-2, 1:-1]
        - 4.0 * centre
    )
    return centre + coeffs[None] * laplace


def exact_dot(left, right, left_dim):
    return lax.dot_general(
        left,
        right,
        (((left_dim,), (0,)), ((), ())),
        precision=lax.Precision.HIGHEST,
        preferred_element_type=jnp.float32,
    )


def per_device(
    adjoint,
    trajectory,
    diffusivity,
    land_mask,
    coriolis,
    obs_values,
    obs_weight,
    obs_owner,
    obs_offset,
    fold_partner,
):
    wet_cells = land_mask.astype(jnp.float32)
    work_state = adjoint * wet_cells[None]
    sign_four = jnp.array([1.0, 1.0, -1.0, -1.0], jnp.float32).reshape(4, 1, 1, 1)
    for sweep_index in range(NSUB):
        extended = rim_cells(work_state, sign_four, fold_partner, 1)
        work_state = mix_step(extended, diffusivity)
    rotation = coriolis[:, None]
    adjoint_u = work_state[2] - rotation * work_state[3]
    adjoint_v = work_state[3] + rotation * work_state[2]
    mixed = jnp.stack([work_state[0], work_state[1], adjoint_u, adjoint_v])
    lon_count = lax.axis_size("lon")
    lat_count = lax.axis_size("lat")
    devices = lon_count * lat_count
    seg_width = obs_values.shape[1]
    rows_sent = obs_values.shape[0]
    owner_index = obs_owner[:, 0]
    one_hot = (owner_index[:, None] == jnp.arange(devices, dtype=jnp.int32)[None, :]).astype(
        jnp.float32
    )
    row_ids = jnp.arange(rows_sent, dtype=jnp.int32)
    before = (row_ids[None, :] < row_ids[:, None]).astype(jnp.float32)
    earlier = exact_dot(before, one_hot, 1)
    slot_index = jnp.sum(earlier * one_hot, axis=1).astype(jnp.int32)
    dest_index = owner_index * CAP + slot_index
    slot_ids = jnp.arange(devices * CAP, dtype=jnp.int32)
    place_hit = dest_index[:, None] == slot_ids[None, :]
    placement = place_hit.astype(jnp.float32)
    send_values = exact_dot(placement, obs_values, 0).reshape(devices, CAP, seg_width)
    send_weight = exact_dot(placement, obs_weight[:, None], 0).reshape(devices, CAP)
    send_offset = jnp.sum(jnp.where(place_hit, obs_offset[:, None], 0), axis=0).reshape(
        devices, CAP
    )
    got_values, got_weight, got_offset = (
        lax.all_to_all(send_values, ("lon", "lat"), split_axis=0, concat_axis=0, tiled=True),
        lax.all_to_all(send_weight, ("lon", "lat"), split_axis=0, concat_axis=0, tiled=True),
        lax.all_to_all(send_offset, ("lon", "lat"), split_axis=0, concat_axis=0, tiled=True),
    )
    got_values = got_values.reshape(devices * CAP, seg_width)
    got_weight = got_weight.reshape(devices * CAP)
    got_offset = got_offset.reshape(devices * CAP)
    traj_rows = trajectory.reshape(-1, seg_width)
    tile_ids = jnp.arange(traj_rows.shape[0], dtype=jnp.int32)
    picker = (got_offset[:, None] == tile_ids[None, :]).astype(jnp.float32)
    sampled = exact_dot(picker, traj_rows, 1)
    misfit = got_weight[:, None] * (sampled - got_values)
    forcing = exact_dot(picker, misfit, 0).reshape(adjoint.shape)
    return wet_cells[None] * (mixed + forcing)


def solution(mesh):
    return jax.shard_map(
        per_device,
        mesh=mesh,
        in_specs=(
            P(None, None, "lat", "lon"),
            P(None, None, "lat", "lon"),
            P(None, "lat", "lon"),
            P(None, "lat", "lon"),
            P("lat"),
            P(("lon", "lat"), None),
            P(("lon", "lat")),
            P(("lon", "lat"), None),
            P(("lon", "lat")),
            P("lon"),
        ),
        out_specs=P(None, None, "lat", "lon"),
        check_vma=False,
    )
```

profile of v0, /device:TPU:28, one launch (start us, length us, event | category | flops | bytes accessed | tf_op | source)
XLA Modules:
  0.0 222.5 jit_solution(14779265512521191120)
XLA Ops:
  3.0 5.8 %all-to-all-start = ((s32[32,1,8]{2,1,0:T(1,128)}), s32[32,1,8]{2,1,0:T(1,128)S(1)}, u32[]{:S(2)}, u32[]{:S(2)}) async-start(s32[32,1,8]{2,1,0:T(1,128)} %bitcast.12), calls=%async_computation | async-start | bytes 32768 | tf_op jit(solution)/shard_map/all_to_all | solution.py:104
  10.3 3.8 %broadcast_multiply_fusion = f32[4,10,64,512]{3,2,1,0:T(8,128)S(1)} fusion(f32[4,10,64,512]{3,2,1,0:T(8,128)} %param.13, f32[10,64,512]{2,1,0:T(8,128)S(1)} %convert_element_type.20), kind=kLoop, calls=%fused_computation.52 | loop fusion | flops 1310720 | bytes 11796480 | tf_op jit(solution)/shard_map/mul | solution.py:70
  14.1 2.3 %copy-done.5 = f32[4,10,64,512]{3,2,1,0:T(8,128)} copy-done((f32[4,10,64,512]{3,2,1,0:T(8,128)}, f32[4,10,64,512]{3,2,1,0:T(8,128)S(1)}, u32[]{:S(2)}) %copy-start.5) | copy-done | bytes 5242904
  18.8 3.5 %collective-permute-start.1 = (f32[4,10,1,512]{3,0,2,1:T(4,128)S(1)}, f32[4,10,1,512]{3,0,2,1:T(4,128)S(1)}, u32[]{:S(2)}, u32[]{:S(2)}) collective-permute-start(f32[4,10,1,512]{3,0,2,1:T(4,128)S(1)} %copy.252), channel_id=1, source_target_pairs={{1,0},{2,1},{3,2},{4,3},{5,4},{6,5},{7,6},{9,8},{10,9},{11,10},{12... | collective-permute-start | bytes 245768 | tf_op jit(solution)/shard_map/ppermute | solution.py:18
  22.3 9.6 %all_gather.9 = f32[4,10,1,2048]{3,0,2,1:T(4,128)S(1)} all-gather(f32[4,10,1,512]{3,0,2,1:T(4,128)S(1)} %copy.247), channel_id=1, replica_groups=mesh['lon'=4,'lat'=8] {'lon'}, dimensions={3}, use_global_device_ids=true | all-gather | bytes 409600 | tf_op jit(solution)/shard_map/all_gather | solution.py:26
  31.9 3.1 %copy.249 = f32[4,10,2048]{1,0,2:T(4,128)} copy(f32[4,10,2048]{2,0,1:T(4,128)S(1)} %bitcast.41) | data formatting | bytes 655360 | tf_op jit(solution)/shard_map/jit(_take)/Arg_0.3 | solution.py:27
  35.0 3.7 %gather_fusion = f32[512,4,10]{2,1,0:T(4,128)S(1)} fusion(f32[4,10,2048]{1,0,2:T(4,128)} %copy.249, s32[1024]{0:T(1024)S(1)} %pad_clamp_fusion), kind=kCustom, calls=%fused_computation.clone | custom fusion | bytes 165888 | tf_op jit(solution)/shard_map/jit(_take)/gather | solution.py:27
  39.3 4.0 %pad_maximum_fusion.32 = (f32[4,10,66,1]{3,2,1,0:T(8,128)}, f32[4,10,66,1]{3,2,1,0:T(8,128)}) fusion(f32[4,10,1,512]{3,2,1,0:T(1,128)S(1)} %broadcast_select_fusion.5, f32[4,10,64,512]{3,2,1,0:T(8,128)} %copy-done.5, f32[4,10,1,512]{3,2,1,0:T(1,128)S(1)} %copy.254), kind=kLoop, calls=%fused_computation.61 | loop fusion | flops 10560 | bytes 5427840 | tf_op jit(solution)/shard_map/slice | solution.py:16
  47.3 2.7 %collective-permute-start.2 = (f32[4,10,66,1]{2,0,3,1:T(4,128)S(1)}, f32[4,10,66,1]{2,0,3,1:T(4,128)S(1)}, u32[]{:S(2)}, u32[]{:S(2)}) collective-permute-start(f32[4,10,66,1]{2,0,3,1:T(4,128)S(1)} %copy.255), channel_id=1, source_target_pairs={{8,0},{16,8},{24,16},{0,24},{9,1},{17,9},{25,17},{1,25},{10,2},{18... | collective-permute-start | bytes 31688 | tf_op jit(solution)/shard_map/ppermute | solution.py:18
  54.9 13.2 %fusion.17 = f32[4,10,64,512]{3,2,1,0:T(8,128)S(1)} fusion(f32[4,10,64,512]{3,2,1,0:T(8,128)} %copy-done.5, f32[4,10,1,512]{3,2,1,0:T(1,128)S(1)} %copy.254, f32[4,10,1,512]{3,2,1,0:T(1,128)S(1)} %broadcast_select_fusion.5, f32[4,10,66,1]{3,2,1,0:T(8,128)} %copy.258, f32[4,10,66,1]{3,2,1,0:T(8,128)} %copy.256, f32[10,64,512]{2,1,0:T(8,128)S(1)} %copy-done.6), kind=kLoop, calls=%fused_computation.38 | loop fusion | flops 19660800 | bytes 11981440 | tf_op jit(solution)/shard_map/add | solution.py:44
  68.1 2.3 %copy-done.2 = f32[4,10,64,512]{3,2,1,0:T(8,128)} copy-done((f32[4,10,64,512]{3,2,1,0:T(8,128)}, f32[4,10,64,512]{3,2,1,0:T(8,128)S(1)}, u32[]{:S(2)}) %copy-start.2) | copy-done | bytes 5242904
  72.6 3.6 %collective-permute-start.5 = (f32[4,10,1,512]{3,0,2,1:T(4,128)S(1)}, f32[4,10,1,512]{3,0,2,1:T(4,128)S(1)}, u32[]{:S(2)}, u32[]{:S(2)}) collective-permute-start(f32[4,10,1,512]{3,0,2,1:T(4,128)S(1)} %copy.265), channel_id=1, source_target_pairs={{1,0},{2,1},{3,2},{4,3},{5,4},{6,5},{7,6},{9,8},{10,9},{11,10},{12... | collective-permute-start | bytes 245768 | tf_op jit(solution)/shard_map/ppermute | solution.py:18
  77.9 9.8 %all_gather.10 = f32[4,10,1,2048]{3,0,2,1:T(4,128)S(1)} all-gather(f32[4,10,1,512]{3,0,2,1:T(4,128)S(1)} %copy.260), channel_id=1, replica_groups=mesh['lon'=4,'lat'=8] {'lon'}, dimensions={3}, use_global_device_ids=true | all-gather | bytes 409600 | tf_op jit(solution)/shard_map/all_gather | solution.py:26
  87.7 3.1 %copy.262 = f32[4,10,2048]{1,0,2:T(4,128)} copy(f32[4,10,2048]{2,0,1:T(4,128)S(1)} %bitcast.42) | data formatting | bytes 655360 | tf_op jit(solution)/shard_map/jit(_take)/Arg_0.3 | solution.py:27
  90.8 3.7 %gather_fusion.1 = f32[512,4,10]{2,1,0:T(4,128)S(1)} fusion(f32[4,10,2048]{1,0,2:T(4,128)} %copy.262, s32[1024]{0:T(1024)S(1)} %pad_clamp_fusion), kind=kCustom, calls=%fused_computation.1.clone | custom fusion | bytes 165888 | tf_op jit(solution)/shard_map/jit(_take)/gather | solution.py:27
  95.1 3.9 %pad_maximum_fusion.29 = (f32[4,10,66,1]{3,2,1,0:T(8,128)}, f32[4,10,66,1]{3,2,1,0:T(8,128)}) fusion(f32[4,10,1,512]{3,2,1,0:T(1,128)S(1)} %broadcast_select_fusion.4, f32[4,10,64,512]{3,2,1,0:T(8,128)} %copy-done.2, f32[4,10,1,512]{3,2,1,0:T(1,128)S(1)} %copy.267), kind=kLoop, calls=%fused_computation.58 | loop fusion | flops 10560 | bytes 5427840 | tf_op jit(solution)/shard_map/slice | solution.py:16
  105.8 5.4 %all-to-all-start.1 = ((f32[32,1,8]{2,1,0:T(1,128)}), f32[32,1,8]{2,1,0:T(1,128)S(1)}, u32[]{:S(2)}, u32[]{:S(2)}) async-start(f32[32,1,8]{2,1,0:T(1,128)} %convolution_bitcast_fusion.1), calls=%async_computation.1 | async-start | bytes 32768 | tf_op jit(solution)/shard_map/all_to_all | solution.py:103
  112.2 6.5 %reshape.71 = f32[10240,128]{1,0:T(8,128)} reshape(f32[4,10,64,512]{3,2,1,0:T(8,128)} %param.14) | data formatting | bytes 10485760 | tf_op jit(solution)/shard_map/reshape | solution.py:109
  119.8 5.8 %all-to-all-start.2 = ((f32[32,8,128]{2,1,0:T(8,128)}), f32[32,8,128]{2,1,0:T(8,128)S(1)}, u32[]{:S(2)}, u32[]{:S(2)}) async-start(f32[32,8,128]{2,1,0:T(8,128)} %convolution_bitcast_fusion), calls=%async_computation.2 | async-start | bytes 262144 | tf_op jit(solution)/shard_map/all_to_all | solution.py:102
  130.5 12.2 %fusion.11 = f32[4,10,64,512]{3,2,1,0:T(8,128)S(1)} fusion(f32[4,10,64,512]{3,2,1,0:T(8,128)} %copy-done.2, f32[4,10,1,512]{3,2,1,0:T(1,128)S(1)} %copy.267, f32[4,10,1,512]{3,2,1,0:T(1,128)S(1)} %broadcast_select_fusion.4, f32[4,10,66,1]{3,2,1,0:T(8,128)} %copy.271, f32[4,10,66,1]{3,2,1,0:T(8,128)} %copy.269, f32[10,64,512]{2,1,0:T(8,128)S(1)} %copy-done.6), kind=kLoop, calls=%fused_computation.24 | loop fusion | flops 19660800 | bytes 11981440 | tf_op jit(solution)/shard_map/add | solution.py:44
  142.7 2.3 %copy-done.3 = f32[4,10,64,512]{3,2,1,0:T(8,128)} copy-done((f32[4,10,64,512]{3,2,1,0:T(8,128)}, f32[4,10,64,512]{3,2,1,0:T(8,128)S(1)}, u32[]{:S(2)}) %copy-start.3) | copy-done | bytes 5242904
  147.3 3.5 %collective-permute-start.9 = (f32[4,10,1,512]{3,0,2,1:T(4,128)S(1)}, f32[4,10,1,512]{3,0,2,1:T(4,128)S(1)}, u32[]{:S(2)}, u32[]{:S(2)}) collective-permute-start(f32[4,10,1,512]{3,0,2,1:T(4,128)S(1)} %copy.278), channel_id=1, source_target_pairs={{1,0},{2,1},{3,2},{4,3},{5,4},{6,5},{7,6},{9,8},{10,9},{11,10},{12... | collective-permute-start | bytes 245768 | tf_op jit(solution)/shard_map/ppermute | solution.py:18
  150.8 9.6 %all_gather.11 = f32[4,10,1,2048]{3,0,2,1:T(4,128)S(1)} all-gather(f32[4,10,1,512]{3,0,2,1:T(4,128)S(1)} %copy.273), channel_id=1, replica_groups=mesh['lon'=4,'lat'=8] {'lon'}, dimensions={3}, use_global_device_ids=true | all-gather | bytes 409600 | tf_op jit(solution)/shard_map/all_gather | solution.py:26
  160.4 3.2 %copy.275 = f32[4,10,2048]{1,0,2:T(4,128)} copy(f32[4,10,2048]{2,0,1:T(4,128)S(1)} %bitcast.43) | data formatting | bytes 655360 | tf_op jit(solution)/shard_map/jit(_take)/Arg_0.3 | solution.py:27
  163.5 3.7 %gather_fusion.2 = f32[512,4,10]{2,1,0:T(4,128)S(1)} fusion(f32[4,10,2048]{1,0,2:T(4,128)} %copy.275, s32[1024]{0:T(1024)S(1)} %pad_clamp_fusion), kind=kCustom, calls=%fused_computation.2.clone | custom fusion | bytes 165888 | tf_op jit(solution)/shard_map/jit(_take)/gather | solution.py:27
  167.6 7.6 %fusion.24 = f32[256,128]{1,0:T(8,128)S(1)} fusion(f32[10240,128]{1,0:T(8,128)} %reshape.71, s32[256]{0:T(256)S(1)} %eq.77, f32[32,8,128]{2,1,0:T(8,128)S(1)} %all-to-all-done.2, f32[256]{0:T(256)S(1)} %mul.118), kind=kOutput, calls=%fused_computation.66 | convolution fusion | flops 4029218816 | bytes 5507072 | tf_op jit(solution)/shard_map/dot_general | solution.py:48
  175.6 2.2 pad_maximum_fusion.26
  181.8 2.7 %collective-permute-start.10 = (f32[4,10,66,1]{2,0,3,1:T(4,128)S(1)}, f32[4,10,66,1]{2,0,3,1:T(4,128)S(1)}, u32[]{:S(2)}, u32[]{:S(2)}) collective-permute-start(f32[4,10,66,1]{2,0,3,1:T(4,128)S(1)} %copy.281), channel_id=1, source_target_pairs={{8,0},{16,8},{24,16},{0,24},{9,1},{17,9},{25,17},{1,25},{10,2},{18... | collective-permute-start | bytes 31688 | tf_op jit(solution)/shard_map/ppermute | solution.py:18
  184.5 10.2 %fusion = f32[10240,128]{1,0:T(8,128)} fusion(f32[256,128]{1,0:T(8,128)S(1)} %fusion.24, s32[256]{0:T(256)S(1)} %eq.77), kind=kOutput, calls=%fused_computation.4 | convolution fusion | flops 4029153280 | bytes 5374976 | tf_op jit(solution)/shard_map/dot_general | solution.py:48
  194.7 6.8 %reshape.74 = f32[4,10,64,512]{3,2,1,0:T(8,128)} reshape(f32[10240,128]{1,0:T(8,128)} %fusion) | data formatting | bytes 10485760 | tf_op jit(solution)/shard_map/reshape | solution.py:114
  204.9 12.4 %fusion.5 = f32[4,10,64,512]{3,2,1,0:T(8,128)S(1)} fusion(f32[4,10,64,512]{3,2,1,0:T(8,128)} %copy-done.3, f32[4,10,1,512]{3,2,1,0:T(1,128)S(1)} %copy.280, f32[4,10,1,512]{3,2,1,0:T(1,128)S(1)} %broadcast_select_fusion.3, f32[4,10,66,1]{3,2,1,0:T(8,128)} %copy.284, f32[4,10,66,1]{3,2,1,0:T(8,128)} %copy.282, f32[10,64,512]{2,1,0:T(8,128)S(1)} %copy-done.6), kind=kLoop, calls=%fused_computation.10 | loop fusion | flops 19660800 | bytes 11981440 | tf_op jit(solution)/shard_map/add | solution.py:44
  218.6 3.9 %fusion.20 = f32[4,10,64,512]{3,2,1,0:T(8,128)} fusion(f32[4,10,64,512]{3,2,1,0:T(8,128)S(1)} %bitcast.37, f32[1,10,64,512]{3,2,1,0:T(8,128)S(1)} %get-tuple-element.13, f32[1,10,64,512]{3,2,1,0:T(8,128)S(1)} %get-tuple-element.12, f32[2,10,64,512]{3,2,1,0:T(8,128)S(1)} %slice.136, f32[10,64,512]{2,1,0:T(8,128)S(1)} %copy-done.8), kind=kLoop, calls=%fused_computation.49 | loop fusion | flops 5242880 | bytes 17039360 | tf_op jit(solution)/shard_map/mul | solution.py:115
  (99 shorter events, 45.9 us)
Async XLA Ops:
  0.0 111.2 %copy-start = (f32[128,128]{1,0:T(8,128)S(1)}, f32[128,128]{1,0:T(8,128)}, u32[]{:S(2)}) copy-start(f32[128,128]{1,0:T(8,128)} %param.18) | copy-start | bytes 196612
  3.0 102.8 %all-to-all-start = ((s32[32,1,8]{2,1,0:T(1,128)}), s32[32,1,8]{2,1,0:T(1,128)S(1)}, u32[]{:S(2)}, u32[]{:S(2)}) async-start(s32[32,1,8]{2,1,0:T(1,128)} %bitcast.12), calls=%async_computation | async-start | bytes 32768 | tf_op jit(solution)/shard_map/all_to_all | solution.py:104
  10.3 3.8 %copy-start.7 = (f32[10,64,512]{2,1,0:T(8,128)}, f32[10,64,512]{2,1,0:T(8,128)S(1)}, u32[]{:S(2)}) copy-start(f32[10,64,512]{2,1,0:T(8,128)S(1)} %convert_element_type.20) | copy-start | bytes 3932164
  10.3 11.9 %copy-start.9 = (s32[512]{0:T(512)S(1)}, s32[512]{0:T(512)}, u32[]{:S(2)}) copy-start(s32[512]{0:T(512)} %param.22) | copy-start | bytes 6148
  14.1 2.4 %copy-start.5 = (f32[4,10,64,512]{3,2,1,0:T(8,128)}, f32[4,10,64,512]{3,2,1,0:T(8,128)S(1)}, u32[]{:S(2)}) copy-start(f32[4,10,64,512]{3,2,1,0:T(8,128)S(1)} %broadcast_multiply_fusion) | copy-start | bytes 15728644
  16.5 22.7 %copy-start.10 = (f32[4]{0:T(128)S(1)}, f32[4]{0:T(128)}, u32[]{:S(2)}) copy-start(f32[4]{0:T(128)} %constant.28.clone) | copy-start | bytes 52
  16.7 22.4 %collective-permute-start = (f32[4,10,1,512]{3,0,2,1:T(4,128)S(1)}, f32[4,10,1,512]{3,0,2,1:T(4,128)S(1)}, u32[]{:S(2)}, u32[]{:S(2)}) collective-permute-start(f32[4,10,1,512]{3,0,2,1:T(4,128)S(1)} %copy.247), channel_id=1, source_target_pairs={{0,1},{1,2},{2,3},{3,4},{4,5},{5,6},{6,7},{8,9},{9,10},{10,11},{11... | collective-permute-start | bytes 245768 | tf_op jit(solution)/shard_map/ppermute | solution.py:17
  18.8 20.4 %collective-permute-start.1 = (f32[4,10,1,512]{3,0,2,1:T(4,128)S(1)}, f32[4,10,1,512]{3,0,2,1:T(4,128)S(1)}, u32[]{:S(2)}, u32[]{:S(2)}) collective-permute-start(f32[4,10,1,512]{3,0,2,1:T(4,128)S(1)} %copy.252), channel_id=1, source_target_pairs={{1,0},{2,1},{3,2},{4,3},{5,4},{6,5},{7,6},{9,8},{10,9},{11,10},{12... | collective-permute-start | bytes 245768 | tf_op jit(solution)/shard_map/ppermute | solution.py:18
  39.3 15.6 %copy-start.6 = (f32[10,64,512]{2,1,0:T(8,128)S(1)}, f32[10,64,512]{2,1,0:T(8,128)}, u32[]{:S(2)}) copy-start(f32[10,64,512]{2,1,0:T(8,128)} %param.15) | copy-start | bytes 3932164
  47.1 6.1 %collective-permute-start.3 = (f32[4,10,66,1]{2,0,3,1:T(4,128)S(1)}, f32[4,10,66,1]{2,0,3,1:T(4,128)S(1)}, u32[]{:S(2)}, u32[]{:S(2)}) collective-permute-start(f32[4,10,66,1]{2,0,3,1:T(4,128)S(1)} %copy.257), channel_id=1, source_target_pairs={{0,8},{8,16},{16,24},{24,0},{1,9},{9,17},{17,25},{25,1},{2,10},{10... | collective-permute-start | bytes 31688 | tf_op jit(solution)/shard_map/ppermute | solution.py:17
  47.3 4.2 %collective-permute-start.2 = (f32[4,10,66,1]{2,0,3,1:T(4,128)S(1)}, f32[4,10,66,1]{2,0,3,1:T(4,128)S(1)}, u32[]{:S(2)}, u32[]{:S(2)}) collective-permute-start(f32[4,10,66,1]{2,0,3,1:T(4,128)S(1)} %copy.255), channel_id=1, source_target_pairs={{8,0},{16,8},{24,16},{0,24},{9,1},{17,9},{25,17},{1,25},{10,2},{18... | collective-permute-start | bytes 31688 | tf_op jit(solution)/shard_map/ppermute | solution.py:18
  54.9 21.3 %copy-start.12 = (f32[128]{0:T(128)S(1)}, f32[128]{0:T(128)}, u32[]{:S(2)}) copy-start(f32[128]{0:T(128)} %param.19) | copy-start | bytes 1540
  68.1 2.3 %copy-start.2 = (f32[4,10,64,512]{3,2,1,0:T(8,128)}, f32[4,10,64,512]{3,2,1,0:T(8,128)S(1)}, u32[]{:S(2)}) copy-start(f32[4,10,64,512]{3,2,1,0:T(8,128)S(1)} %fusion.17) | copy-start | bytes 15728644
  70.6 24.2 %collective-permute-start.4 = (f32[4,10,1,512]{3,0,2,1:T(4,128)S(1)}, f32[4,10,1,512]{3,0,2,1:T(4,128)S(1)}, u32[]{:S(2)}, u32[]{:S(2)}) collective-permute-start(f32[4,10,1,512]{3,0,2,1:T(4,128)S(1)} %copy.260), channel_id=1, source_target_pairs={{0,1},{1,2},{2,3},{3,4},{4,5},{5,6},{6,7},{8,9},{9,10},{10,11},{11... | collective-permute-start | bytes 245768 | tf_op jit(solution)/shard_map/ppermute | solution.py:17
  72.6 22.4 %collective-permute-start.5 = (f32[4,10,1,512]{3,0,2,1:T(4,128)S(1)}, f32[4,10,1,512]{3,0,2,1:T(4,128)S(1)}, u32[]{:S(2)}, u32[]{:S(2)}) collective-permute-start(f32[4,10,1,512]{3,0,2,1:T(4,128)S(1)} %copy.265), channel_id=1, source_target_pairs={{1,0},{2,1},{3,2},{4,3},{5,4},{6,5},{7,6},{9,8},{10,9},{11,10},{12... | collective-permute-start | bytes 245768 | tf_op jit(solution)/shard_map/ppermute | solution.py:18
  102.8 25.9 %collective-permute-start.7 = (f32[4,10,66,1]{2,0,3,1:T(4,128)S(1)}, f32[4,10,66,1]{2,0,3,1:T(4,128)S(1)}, u32[]{:S(2)}, u32[]{:S(2)}) collective-permute-start(f32[4,10,66,1]{2,0,3,1:T(4,128)S(1)} %copy.270), channel_id=1, source_target_pairs={{0,8},{8,16},{16,24},{24,0},{1,9},{9,17},{17,25},{25,1},{2,10},{10... | collective-permute-start | bytes 31688 | tf_op jit(solution)/shard_map/ppermute | solution.py:17
  104.8 22.2 %collective-permute-start.6 = (f32[4,10,66,1]{2,0,3,1:T(4,128)S(1)}, f32[4,10,66,1]{2,0,3,1:T(4,128)S(1)}, u32[]{:S(2)}, u32[]{:S(2)}) collective-permute-start(f32[4,10,66,1]{2,0,3,1:T(4,128)S(1)} %copy.268), channel_id=1, source_target_pairs={{8,0},{16,8},{24,16},{0,24},{9,1},{17,9},{25,17},{1,25},{10,2},{18... | collective-permute-start | bytes 31688 | tf_op jit(solution)/shard_map/ppermute | solution.py:18
  105.8 14.0 %all-to-all-start.1 = ((f32[32,1,8]{2,1,0:T(1,128)}), f32[32,1,8]{2,1,0:T(1,128)S(1)}, u32[]{:S(2)}, u32[]{:S(2)}) async-start(f32[32,1,8]{2,1,0:T(1,128)} %convolution_bitcast_fusion.1), calls=%async_computation.1 | async-start | bytes 32768 | tf_op jit(solution)/shard_map/all_to_all | solution.py:103
  119.8 47.8 %all-to-all-start.2 = ((f32[32,8,128]{2,1,0:T(8,128)}), f32[32,8,128]{2,1,0:T(8,128)S(1)}, u32[]{:S(2)}, u32[]{:S(2)}) async-start(f32[32,8,128]{2,1,0:T(8,128)} %convolution_bitcast_fusion), calls=%async_computation.2 | async-start | bytes 262144 | tf_op jit(solution)/shard_map/all_to_all | solution.py:102
  142.7 2.3 %copy-start.3 = (f32[4,10,64,512]{3,2,1,0:T(8,128)}, f32[4,10,64,512]{3,2,1,0:T(8,128)S(1)}, u32[]{:S(2)}) copy-start(f32[4,10,64,512]{3,2,1,0:T(8,128)S(1)} %fusion.11) | copy-start | bytes 15728644
  145.2 30.0 %collective-permute-start.8 = (f32[4,10,1,512]{3,0,2,1:T(4,128)S(1)}, f32[4,10,1,512]{3,0,2,1:T(4,128)S(1)}, u32[]{:S(2)}, u32[]{:S(2)}) collective-permute-start(f32[4,10,1,512]{3,0,2,1:T(4,128)S(1)} %copy.273), channel_id=1, source_target_pairs={{0,1},{1,2},{2,3},{3,4},{4,5},{5,6},{6,7},{8,9},{9,10},{10,11},{11... | collective-permute-start | bytes 245768 | tf_op jit(solution)/shard_map/ppermute | solution.py:17
  147.3 28.1 %collective-permute-start.9 = (f32[4,10,1,512]{3,0,2,1:T(4,128)S(1)}, f32[4,10,1,512]{3,0,2,1:T(4,128)S(1)}, u32[]{:S(2)}, u32[]{:S(2)}) collective-permute-start(f32[4,10,1,512]{3,0,2,1:T(4,128)S(1)} %copy.278), channel_id=1, source_target_pairs={{1,0},{2,1},{3,2},{4,3},{5,4},{6,5},{7,6},{9,8},{10,9},{11,10},{12... | collective-permute-start | bytes 245768 | tf_op jit(solution)/shard_map/ppermute | solution.py:18
  167.6 7.9 %copy-start.4 = (f32[4,10,64,512]{3,2,1,0:T(8,128)S(1)}, f32[4,10,64,512]{3,2,1,0:T(8,128)}, u32[]{:S(2)}) copy-start(f32[4,10,64,512]{3,2,1,0:T(8,128)} %copy-done.3) | copy-start | bytes 15728644
  181.6 21.6 %collective-permute-start.11 = (f32[4,10,66,1]{2,0,3,1:T(4,128)S(1)}, f32[4,10,66,1]{2,0,3,1:T(4,128)S(1)}, u32[]{:S(2)}, u32[]{:S(2)}) collective-permute-start(f32[4,10,66,1]{2,0,3,1:T(4,128)S(1)} %copy.283), channel_id=1, source_target_pairs={{0,8},{8,16},{16,24},{24,0},{1,9},{9,17},{17,25},{25,1},{2,10},{10... | collective-permute-start | bytes 31688 | tf_op jit(solution)/shard_map/ppermute | solution.py:17
  181.8 19.7 %collective-permute-start.10 = (f32[4,10,66,1]{2,0,3,1:T(4,128)S(1)}, f32[4,10,66,1]{2,0,3,1:T(4,128)S(1)}, u32[]{:S(2)}, u32[]{:S(2)}) collective-permute-start(f32[4,10,66,1]{2,0,3,1:T(4,128)S(1)} %copy.281), channel_id=1, source_target_pairs={{8,0},{16,8},{24,16},{0,24},{9,1},{17,9},{25,17},{1,25},{10,2},{18... | collective-permute-start | bytes 31688 | tf_op jit(solution)/shard_map/ppermute | solution.py:18
  203.2 15.1 %slice-start = ((s8[5242880]{0:T(1024)(128)(4,1)}), s8[1048576]{0:T(1024)(128)(4,1)S(1)}, s32[]{:S(2)}) async-start(s8[5242880]{0:T(1024)(128)(4,1)} %bitcast.36), calls=%async_computation.3 | async-start | bytes 2097152
  204.9 13.5 %slice-start.1 = ((s8[5242880]{0:T(1024)(128)(4,1)}), s8[4194304]{0:T(1024)(128)(4,1)S(1)}, s32[]{:S(2)}) async-start(s8[5242880]{0:T(1024)(128)(4,1)} %bitcast.36), calls=%async_computation.4 | async-start | bytes 8388608
  217.3 0.7 copy-start.11
  217.3 1.3 copy-start.8
  218.3 4.1 %copy-start.1 = (f32[128,128]{1,0:T(8,128)S(1)}, f32[128,128]{1,0:T(8,128)}, u32[]{:S(2)}) copy-start(f32[128,128]{1,0:T(8,128)} %param.18) | copy-start | bytes 196612
where the time goes:
time: 224 us; the launch traced here: 222 us
  local copies, waits for them, and re-layouts  66.9 us (30%)
  other arithmetic  60.5 us (27%)
  starting transfers between devices  42.6 us (19%)
  blocking collectives  29 us (13%)
  matrix products  21.4 us (10%)
    add x3, other arithmetic, mix_step(): return centre + coeffs[None] * laplace  37.8 us
    all_gather x3, blocking collectives, rim_cells(): whole_top = lax.all_gather(top_rows, 'lon', axis=3, tiled=True)  29 us
    dot_general x5, matrix products, exact_dot(): lax.dot_general(left, right, (((left_dim,), (0,)), ((), ())), precision=l...  21.4 us
    ppermute x6, starting transfers between devices, padded_2(): after = lax.ppermute(initial, axis, down)  17.1 us
    gather x6, local copies, waits for them, and re-layouts, rim_cells(): jnp.take(whole_top[:, :, ::-1, :], fold_partner, axis=3)  12.2 us
    slice x3, other arithmetic, padded_2(): initial = lax.slice_in_dim(shard, 0, width, axis=dim)  10.1 us
    another operation x3, local copies, waits for them, and re-layouts, rim_cells(): jnp.take(whole_top[:, :, ::-1, :], fold_partner, axis=3)  9.3 us
    ppermute x6, starting transfers between devices, padded_2(): before = lax.ppermute(last, axis, up)  8.45 us
  transfers between devices with their start and end apart: 15, of which 1 were waited for; matrix products, arithmetic and copies ran while one was open for 51% of the time, Pallas kernels for 0%

commit v1 on v0

v1 whole, which is shorter than its diff:
```python
import functools

import jax
import jax.numpy as jnp
from jax import lax
from jax.experimental import pallas as pl
from jax.experimental.pallas import tpu as pltpu
from jax.sharding import PartitionSpec as P

NSUB = 3
CAP = 8
LANES = 128
MESH = pl.DeviceIdType.MESH
VMEM = pltpu.VMEM
F32 = jnp.float32


def dot(left, right, dims, precision=lax.Precision.HIGHEST):
    return lax.dot_general(
        left, right, (dims, ((), ())), precision=precision, preferred_element_type=F32
    )


def pack_kernel(
    n, levels,
    adj_top, adj_bot, adj_w, adj_e, wet_top, wet_bot, wet_w, wet_e,
    dif_top, dif_bot, dif_w, dif_e, owner, weight, offset, values,
    row_top, row_bot, col_w, col_e, obs,
):
    layers = adj_top.shape[0]
    for out in (row_top, row_bot):
        out[...] = jnp.zeros_like(out)

    def state_level(layer, carry):
        k = lax.rem(layer, levels)
        top = adj_top[layer] * wet_top[k].astype(F32)
        bot = adj_bot[layer] * wet_bot[k].astype(F32)
        for r in range(NSUB):
            row_top[r, pl.ds(layer, 1), :] = top[8 - NSUB + r : 8 - NSUB + r + 1]
            row_bot[r, pl.ds(layer, 1), :] = bot[r : r + 1]
        return columns(
            layer, adj_w[layer] * wet_w[k].astype(F32), adj_e[layer] * wet_e[k].astype(F32), carry
        )

    def columns(place, west, east, carry):
        lane = lax.broadcasted_iota(jnp.int32, west.shape, 1)
        first = NSUB * place
        here = (lane >= first) & (lane < first + NSUB)
        west = pltpu.roll(west, first, 1)
        east = pltpu.roll(east, lax.rem(first + NSUB, LANES), 1)
        return jnp.where(here, west, carry[0]), jnp.where(here, east, carry[1])

    def dif_level(k, carry):
        top, bot = dif_top[k], dif_bot[k]
        for r in range(NSUB):
            row_top[r, pl.ds(layers + k, 1), :] = top[8 - NSUB + r : 8 - NSUB + r + 1]
            row_bot[r, pl.ds(layers + k, 1), :] = bot[r : r + 1]
        return columns(k, dif_w[k], dif_e[k], carry)

    zero = jnp.zeros(adj_w.shape[1:], F32)
    west, east = lax.fori_loop(0, layers, state_level, (zero, zero))
    col_w[:, :LANES], col_e[:, :LANES] = west, east
    west, east = lax.fori_loop(0, levels, dif_level, (zero, zero))
    col_w[:, LANES:], col_e[:, LANES:] = west, east

    rows = values.shape[0]
    own = owner[...]
    one_hot = (lax.broadcasted_iota(jnp.int32, (n, rows), 0) == own).astype(F32)
    earlier_than = (
        lax.broadcasted_iota(jnp.int32, (rows, rows), 0)
        < lax.broadcasted_iota(jnp.int32, (rows, rows), 1)
    ).astype(F32)
    earlier = dot(one_hot, earlier_than, ((1,), (0,)), lax.Precision.DEFAULT)
    slot = jnp.sum(earlier * one_hot, axis=0, keepdims=True).astype(jnp.int32)
    dest = own * CAP + slot
    hit = lax.broadcasted_iota(jnp.int32, (n * CAP, rows), 0) == dest
    sent = dot(hit.astype(F32), values[...], ((1,), (0,)))
    w = jnp.sum(jnp.where(hit, weight[...], 0.0), axis=1, keepdims=True)
    o = jnp.sum(jnp.where(hit, offset[...].astype(F32), 0.0), axis=1, keepdims=True)
    lane = lax.broadcasted_iota(jnp.int32, (n * CAP, LANES), 1)
    meta = jnp.where(lane == 0, w, o)
    obs[:, :CAP, :] = sent.reshape(n, CAP, LANES)
    obs[:, CAP:, :] = meta.reshape(n, CAP, LANES)


def exchange_kernel(
    n_lon, n_lat,
    row_top, row_bot, col_w, col_e, obs,
    north, south, west, east, corner_nw, corner_ne, corner_sw, corner_se, fold, got,
    send_sem, recv_sem, fold_send, fold_recv, obs_send, obs_recv, local_sem,
):
    n = n_lon * n_lat
    lon, lat = lax.axis_index("lon"), lax.axis_index("lat")
    me = lon * n_lat + lat
    right, left = lax.rem(lon + 1, n_lon), lax.rem(lon + n_lon - 1, n_lon)
    low, high = lat == 0, lat == n_lat - 1
    up, down = lax.rem(lat + 1, n_lat), lax.rem(lat + n_lat - 1, n_lat)

    barrier = pltpu.get_barrier_semaphore()

    @pl.loop(1, n)
    def _(step):
        peer = lax.rem(me + step, n)
        pl.semaphore_signal(
            barrier, inc=1, device_id=(peer // n_lat, lax.rem(peer, n_lat)), device_id_type=MESH
        )

    pl.semaphore_wait(barrier, n - 1)

    def remote(src, dst, sems, rsems, i, target):
        return pltpu.make_async_remote_copy(
            src_ref=src, dst_ref=dst, send_sem=sems.at[i], recv_sem=rsems.at[i],
            device_id=target, device_id_type=MESH,
        )

    halo = functools.partial(
        lambda i, src, dst, target: remote(src, dst, send_sem, recv_sem, i, target)
    )
    last = col_w.shape[0] - 8
    lifted = [
        halo(0, row_top, south, (lon, up)),
        halo(1, col_e.at[pl.ds(last, 8)], corner_sw, (right, up)),
        halo(2, col_w.at[pl.ds(last, 8)], corner_se, (left, up)),
    ]
    lowered = [
        halo(3, row_bot, north, (lon, down)),
        halo(4, col_e.at[pl.ds(0, 8)], corner_nw, (right, down)),
        halo(5, col_w.at[pl.ds(0, 8)], corner_ne, (left, down)),
    ]
    level = [halo(6, col_e, west, (right, lat)), halo(7, col_w, east, (left, lat))]

    def fold_copy(step, slot):
        peer = lax.rem(lon + step, n_lon)
        return remote(row_top, fold.at[slot], fold_send, fold_recv, step, (peer, lat))

    def obs_copy(step, slot):
        peer = lax.rem(me + step, n)
        return remote(
            obs.at[peer], got.at[slot], obs_send, obs_recv, step,
            (peer // n_lat, lax.rem(peer, n_lat)),
        )

    own_fold = pltpu.make_async_copy(row_top, fold.at[lon], local_sem.at[0])
    own_obs = pltpu.make_async_copy(obs.at[me], got.at[me], local_sem.at[1])

    @pl.when(high)
    def _():
        for step in range(1, n_lon):
            fold_copy(step, lon).start()
        own_fold.start()

    @pl.when(jnp.logical_not(high))
    def _():
        for copy in lifted:
            copy.start()

    @pl.when(jnp.logical_not(low))
    def _():
        for copy in lowered:
            copy.start()

    for copy in level:
        copy.start()

    @pl.loop(1, n)
    def _(step):
        obs_copy(step, me).start()

    own_obs.start()

    @pl.when(high)
    def _():
        for step in range(1, n_lon):
            fold_copy(step, lax.rem(lon + n_lon - step, n_lon)).wait_recv()
            fold_copy(step, lon).wait_send()
        own_fold.wait()

    @pl.when(jnp.logical_not(high))
    def _():
        for copy in lifted:
            copy.wait_send()
        for copy in lowered:
            copy.wait_recv()

    @pl.when(jnp.logical_not(low))
    def _():
        for copy in lowered:
            copy.wait_send()
        for copy in lifted:
            copy.wait_recv()

    for copy in level:
        copy.wait()

    @pl.loop(1, n)
    def _(step):
        obs_copy(step, lax.rem(me + n - step, n)).wait_recv()
        obs_copy(step, me).wait_send()

    own_obs.wait()


def main_kernel(
    n, n_lon, n_lat, layers,
    got_offset, got_weight, partner,
    adj, dif, wet_ref, coriolis, traj, got,
    north, south, west, east, corner_nw, corner_ne, corner_sw, corner_se, fold,
    out, forcing, rim, ext,
):
    k = pl.program_id(0)
    fields, _, cy, cx = adj.shape
    levels = layers // fields
    lat = lax.axis_index("lat")
    low, high = lat == 0, lat == n_lat - 1
    wide = cx + LANES
    segs = cx // LANES
    sub8 = lax.broadcasted_iota(jnp.int32, (8, LANES), 0)

    @pl.when(k == 0)
    def _():
        forcing[...] = jnp.zeros_like(forcing)
        ext[...] = jnp.zeros_like(ext)

        @pl.loop(0, n)
        def _(block):
            for s in range(CAP):
                place = got_offset[block * CAP + s]
                lanes = pl.ds(pl.multiple_of(lax.rem(place, segs) * LANES, LANES), LANES)
                rest = place // segs
                y, layer = lax.rem(rest, cy), rest // cy
                tile = pl.ds(pl.multiple_of(y // 8 * 8, 8), 8)
                misfit = got_weight[block * CAP + s] * (
                    traj[layer, tile, lanes] - got[block, s : s + 1, :]
                )
                forcing[layer, tile, lanes] = forcing[layer, tile, lanes] + jnp.where(
                    sub8 == lax.rem(y, 8), misfit, 0.0
                )

        @pl.when(jnp.logical_not(high))
        def _():
            rim[:, :, :cx] = north[...]

        @pl.when(high)
        def _():
            nx = n_lon * cx
            lane = lax.broadcasted_iota(jnp.int32, (cx, wide), 1)
            lane = jnp.where(lane < cx + LANES // 2, lane, lane - wide)
            column = partner[0] - lane
            column = jnp.where(column < 0, column + nx, column)
            column = jnp.where(column >= nx, column - nx, column)
            within = lax.broadcasted_iota(jnp.int32, (cx, wide), 0)
            for r in range(NSUB):
                total = jnp.zeros((fold.shape[2], wide), F32)
                for t in range(n_lon):
                    pick = (within + t * cx == column).astype(F32).astype(jnp.bfloat16)
                    left = fold[t, NSUB - 1 - r]
                    for part in range(3):
                        piece = left.astype(jnp.bfloat16)
                        left = left - piece.astype(F32)
                        total = total + dot(piece, pick, ((1,), (0,)), None)
                rim[r] = total

    lane = lax.broadcasted_iota(jnp.int32, (cy, LANES), 1)
    lane8 = lax.broadcasted_iota(jnp.int32, (8, LANES), 1)

    def surround(place, row, side, sign):
        cols = pl.ds(side * LANES, LANES)
        shift_e = lax.rem(LANES - NSUB * place, LANES)
        shift_w = lax.rem(2 * LANES - NSUB - NSUB * place, LANES)
        ext[:cy, cx:] = jnp.where(
            lane < LANES // 2,
            pltpu.roll(east[:, cols], shift_e, 1),
            pltpu.roll(west[:, cols], shift_w, 1),
        )

        def corner(e_ref, w_ref, absent):
            both = jnp.where(
                lane8 < LANES // 2,
                pltpu.roll(e_ref[:, cols], shift_e, 1),
                pltpu.roll(w_ref[:, cols], shift_w, 1),
            )
            return jnp.where(absent, 0.0, both)

        ext[cy:, cx:] = jnp.where(
            sub8 < 4,
            corner(corner_ne, corner_nw, high),
            corner(corner_se, corner_sw, low),
        )
        for r in range(NSUB):
            ext[cy + r : cy + r + 1, :cx] = sign * rim[r, pl.ds(row, 1), :][:, :cx]
            line = south[r, pl.ds(row, 1), :]
            at = cy + 8 - NSUB + r
            ext[at : at + 1, :cx] = jnp.where(low, 0.0, line)

        @pl.when(high)
        def _():
            for r in range(NSUB):
                ext[cy + r : cy + r + 1, cx:] = sign * rim[r, pl.ds(row, 1), :][:, cx:]

    ext[:cy, :cx] = dif[0]
    surround(k, layers + k, 1, 1.0)
    coeffs = ext[...]
    wet = wet_ref[0].astype(F32)
    mixed = []
    for f in range(fields):
        ext[:cy, :cx] = adj[f, 0] * wet
        layer = f * levels + k
        surround(layer, layer, 0, jnp.where(high, 1.0 if f < 2 else -1.0, 1.0))
        work = ext[...]
        for _ in range(NSUB):
            near = (
                pltpu.roll(work, wide - 1, 1)
                + pltpu.roll(work, 1, 1)
                + pltpu.roll(work, cy + 7, 0)
                + pltpu.roll(work, 1, 0)
            )
            work = work + coeffs * (near - 4.0 * work)
        mixed.append(work[:cy, :cx])
    line = coriolis[...]
    square = lax.broadcasted_iota(jnp.int32, (cy, cy), 0) == lax.broadcasted_iota(
        jnp.int32, (cy, cy), 1
    )
    turn = jnp.sum(jnp.where(square, line, 0.0), axis=1, keepdims=True)
    u, v = mixed[2] - turn * mixed[3], mixed[3] + turn * mixed[2]
    for f, m in enumerate((mixed[0], mixed[1], u, v)):
        out[f, 0] = wet * (m + forcing[f * levels + k])


def per_device(
    n_lon, n_lat,
    adjoint, trajectory, diffusivity, land_mask, coriolis,
    obs_values, obs_weight, obs_owner, obs_offset, fold_partner,
):
    n = n_lon * n_lat
    fields, levels, cy, cx = adjoint.shape
    layers = fields * levels
    rows = obs_values.shape[0]
    adj3 = adjoint.reshape(layers, cy, cx)
    traj3 = trajectory.reshape(layers, cy, cx)

    def edges(depth):
        top = pl.BlockSpec((depth, 8, cx), lambda i: (0, cy // 8 - 1, 0))
        bot = pl.BlockSpec((depth, 8, cx), lambda i: (0, 0, 0))
        west = pl.BlockSpec((depth, cy, LANES), lambda i: (0, 0, 0))
        east = pl.BlockSpec((depth, cy, LANES), lambda i: (0, 0, cx // LANES - 1))
        return [top, bot, west, east]

    def whole(shape):
        return pl.BlockSpec(shape, lambda i: (0,) * len(shape))

    def f32(*shape):
        return jax.ShapeDtypeStruct(shape, F32)

    packed = -(-(layers + levels) // 8) * 8
    row_shape, col_shape, obs_shape = (NSUB, packed, cx), (cy, 2 * LANES), (n, 2 * CAP, LANES)
    shapes = [row_shape, row_shape, col_shape, col_shape, obs_shape]
    packs = pl.pallas_call(
        functools.partial(pack_kernel, n, levels),
        grid=(1,),
        out_shape=[f32(*s) for s in shapes],
        in_specs=edges(layers) + edges(levels) + edges(levels)
        + [whole((1, rows))] * 3 + [whole((rows, LANES))],
        out_specs=[whole(s) for s in shapes],
        compiler_params=pltpu.CompilerParams(vmem_limit_bytes=48 << 20),
        name="pack",
    )(
        *[adj3] * 4, *[land_mask] * 4, *[diffusivity] * 4,
        obs_owner.reshape(1, rows), obs_weight.reshape(1, rows), obs_offset.reshape(1, rows),
        obs_values,
    )

    corner = (8, 2 * LANES)
    came = [row_shape, row_shape, col_shape, col_shape, corner, corner, corner, corner]
    fold_shape = (n_lon,) + row_shape
    *halos, fold, got = pl.pallas_call(
        functools.partial(exchange_kernel, n_lon, n_lat),
        out_shape=[f32(*s) for s in came + [fold_shape, obs_shape]],
        in_specs=[pl.BlockSpec(memory_space=pl.ANY)] * 5,
        out_specs=[pl.BlockSpec(memory_space=pl.ANY)] * 10,
        scratch_shapes=[
            pltpu.SemaphoreType.DMA((8,)), pltpu.SemaphoreType.DMA((8,)),
            pltpu.SemaphoreType.DMA((n_lon,)), pltpu.SemaphoreType.DMA((n_lon,)),
            pltpu.SemaphoreType.DMA((n,)), pltpu.SemaphoreType.DMA((n,)),
            pltpu.SemaphoreType.DMA((2,)),
        ],
        compiler_params=pltpu.CompilerParams(collective_id=0, has_side_effects=True),
        name="exchange",
    )(*packs)

    got_weight = got[:, CAP:, 0].reshape(n * CAP)
    got_offset = got[:, CAP:, 1].reshape(n * CAP).astype(jnp.int32)
    smem = pl.BlockSpec(memory_space=pltpu.SMEM)
    level3 = pl.BlockSpec((1, cy, cx), lambda i: (i, 0, 0))
    level4 = pl.BlockSpec((fields, 1, cy, cx), lambda i: (0, i, 0, 0))
    return pl.pallas_call(
        functools.partial(main_kernel, n, n_lon, n_lat, layers),
        grid=(levels,),
        out_shape=f32(*adjoint.shape),
        in_specs=[smem, smem, smem, level4, level3, level3, whole((1, cy)),
                  whole((layers, cy, cx)), whole(obs_shape)]
        + [whole(s) for s in came] + [whole(fold_shape)],
        out_specs=level4,
        scratch_shapes=[
            VMEM((layers, cy, cx), F32),
            VMEM((NSUB, packed, cx + LANES), F32),
            VMEM((cy + 8, cx + LANES), F32),
        ],
        compiler_params=pltpu.CompilerParams(vmem_limit_bytes=56 << 20),
        name="mix",
    )(
        got_offset, got_weight, fold_partner, adjoint, diffusivity, land_mask,
        coriolis.reshape(1, cy), traj3, got, *halos, fold,
    )


def solution(mesh):
    return jax.shard_map(
        functools.partial(per_device, mesh.shape["lon"], mesh.shape["lat"]),
        mesh=mesh,
        in_specs=(
            P(None, None, "lat", "lon"),
            P(None, None, "lat", "lon"),
            P(None, "lat", "lon"),
            P(None, "lat", "lon"),
            P("lat"),
            P(("lon", "lat"), None),
            P(("lon", "lat")),
            P(("lon", "lat"), None),
            P(("lon", "lat")),
            P("lon"),
        ),
        out_specs=P(None, None, "lat", "lon"),
        check_vma=False,
    )
```

time: 224 us -> 77 us (0.34)
  the two profiles are of different devices: /device:TPU:28 before, /device:TPU:27 now
where the time goes in v1:
time: 77 us; the launch traced here: 76.7 us
  Pallas kernels  63.9 us (83%)
  local copies, waits for them, and re-layouts  11.1 us (14%)
  other arithmetic  1.59 us (2%)
    pallas_call x1, Pallas kernels, per_device(): pl.pallas_call(functools.partial(main_kernel, n, n_lon, n_lat, layers), g...  37.6 us
    pallas_call x1, Pallas kernels, per_device(): pl.pallas_call(functools.partial(exchange_kernel, n_lon, n_lat), out_shap...  19.2 us
    unnamed x22, local copies, waits for them, and re-layouts  8.83 us
    pallas_call x1, Pallas kernels, per_device(): pl.pallas_call(functools.partial(pack_kernel, n, levels), grid=(1,), out_...  7.11 us
    convert_element_type x1, other arithmetic, per_device(): got_offset = got[:, CAP:, 1].reshape(n * CAP).astype(jnp.int32)  1.59 us

profile of v1, /device:TPU:27, one launch (start us, length us, event | category | flops | bytes accessed | tf_op | source)
XLA Modules:
  0.0 76.7 jit_solution(14878913569492849651)
XLA Ops:
  0.0 0.0 copy-start
  0.0 1.3 %copy-done = s32[10,64,512]{2,1,0:T(8,128)S(1)} copy-done((s32[10,64,512]{2,1,0:T(8,128)S(1)}, s32[10,64,512]{2,1,0:T(8,128)}, u32[]{:S(2)}) %copy-start) | copy-done | bytes 1310744
  1.3 0.0 copy-start.1
  1.3 1.3 %copy-done.1 = f32[10,64,512]{2,1,0:T(8,128)S(1)} copy-done((f32[10,64,512]{2,1,0:T(8,128)S(1)}, f32[10,64,512]{2,1,0:T(8,128)}, u32[]{:S(2)}) %copy-start.1) | copy-done | bytes 1310744
  2.6 0.0 copy-start.5
  2.6 0.8 %copy-done.5 = f32[128,128]{1,0:T(8,128)S(1)} copy-done((f32[128,128]{1,0:T(8,128)S(1)}, f32[128,128]{1,0:T(8,128)}, u32[]{:S(2)}) %copy-start.5) | copy-done | bytes 65560
  3.5 0.0 copy-start.8
  3.5 0.7 copy-done.8
  4.1 0.0 copy-start.9
  4.1 0.7 copy-done.9
  4.8 0.0 copy-start.10
  4.8 0.7 copy-done.10
  5.4 7.1 %pack.1 = (f32[3,56,512]{2,1,0:T(8,128)S(1)}, f32[3,56,512]{2,1,0:T(8,128)S(1)}, f32[64,256]{1,0:T(8,128)S(1)}, f32[64,256]{1,0:T(8,128)S(1)}, f32[32,16,128]{2,1,0:T(8,128)S(1)}) custom-call(f32[40,64,512]{2,1,0:T(8,128)} %bitcast.9, f32[40,64,512]{2,1,0:T(8,128)} %bitcast.10, f32[40,64,512]{2,1,0:T(8,128)} %bitcast.11, f32[40,64,512]{2,1,0:T(8,128)} %bitcast.12, ...), custom_call_target="tpu_custom_call" | custom-call | tf_op jit(solution)/shard_map/pack/pallas_call | solution.py:357
  12.6 0.0 copy-start.2
  12.6 0.7 copy-done.2
  13.3 0.0 copy-start.3
  13.3 0.7 copy-done.3
  14.0 0.0 copy-start.4
  14.0 0.7 copy-done.4
  14.7 0.0 copy-start.6
  14.7 0.6 copy-done.6
  15.3 0.0 copy-start.7
  15.3 0.6 copy-done.7
  16.0 19.2 %exchange.1 = (f32[3,56,512]{2,1,0:T(8,128)}, f32[3,56,512]{2,1,0:T(8,128)}, f32[64,256]{1,0:T(8,128)}, f32[64,256]{1,0:T(8,128)}, f32[8,256]{1,0:T(8,128)}, /*i...) custom-call(f32[3,56,512]{2,1,0:T(8,128)} %copy-done.2, ...), custom_call_target="tpu_custom_call" | custom-call | tf_op jit(solution)/shard_map/exchange/pallas_call | solution.py:375
  35.1 1.0 %slice_reduce_fusion = f32[32,8]{1,0:T(8,128)S(1)} fusion(f32[32,16,128]{2,1,0:T(8,128)} %get-tuple-element.25.got), kind=kLoop, calls=%fused_computation | loop fusion | bytes 2048 | tf_op jit(solution)/shard_map/slice | solution.py:390
  36.2 0.7 reshape_squeeze.4.got_weight
  36.8 1.6 %convert_reduce_fusion = s32[32,8]{1,0:T(8,128)S(1)} fusion(f32[32,16,128]{2,1,0:T(8,128)} %get-tuple-element.25.got), kind=kLoop, calls=%fused_computation.1 | loop fusion | flops 256 | bytes 2048 | tf_op jit(solution)/shard_map/convert_element_type | solution.py:391
  38.4 0.6 convert_element_type.6.got_offset
  39.1 37.6 %mix.1 = f32[4,10,64,512]{3,2,1,0:T(8,128)} custom-call(s32[256]{0:T(256)} %convert_element_type.6.got_offset, f32[256]{0:T(256)} %reshape_squeeze.4.got_weight, s32[512]{0:T(512)} %partner.1, f32[4,10,64,512]{3,2,1,0:T(8,128)} %adj.1, f32[10,64,512]{2,1,0:T(8,128)} %dif.1, s32[10,64,512]{2,1,0:T(8,128)} %wet_ref.1, f32[1,64]{1,0:T(1,128)} %bitcast.14, ...), custom_call_target="tpu_custom_call" | custom-call | tf_op jit(solution)/shard_map/mix/pallas_call | solution.py:395
Async XLA Ops:
  0.0 1.3 %copy-start = (s32[10,64,512]{2,1,0:T(8,128)S(1)}, s32[10,64,512]{2,1,0:T(8,128)}, u32[]{:S(2)}) copy-start(s32[10,64,512]{2,1,0:T(8,128)} %wet_ref.1) | copy-start | bytes 3932164
  1.3 1.3 %copy-start.1 = (f32[10,64,512]{2,1,0:T(8,128)S(1)}, f32[10,64,512]{2,1,0:T(8,128)}, u32[]{:S(2)}) copy-start(f32[10,64,512]{2,1,0:T(8,128)} %dif.1) | copy-start | bytes 3932164
  2.6 0.8 %copy-start.5 = (f32[128,128]{1,0:T(8,128)S(1)}, f32[128,128]{1,0:T(8,128)}, u32[]{:S(2)}) copy-start(f32[128,128]{1,0:T(8,128)} %values.1) | copy-start | bytes 196612
  3.5 0.7 copy-start.8
  4.1 0.7 copy-start.9
  4.8 0.7 copy-start.10
  12.6 0.7 copy-start.2
  13.3 0.7 copy-start.3
  14.0 0.7 copy-start.4
  14.7 0.6 copy-start.6
  15.3 0.6 copy-start.7

commit v2 on v1

--- a/solution.py
+++ b/solution.py
@@ -202,7 +202,7 @@
 
 def main_kernel(
     n, n_lon, n_lat, layers,
-    got_offset, got_weight, partner,
+    meta, partner,
     adj, dif, wet_ref, coriolis, traj, got,
     north, south, west, east, corner_nw, corner_ne, corner_sw, corner_se, fold,
     out, forcing, rim, ext,
@@ -224,12 +224,12 @@
         @pl.loop(0, n)
         def _(block):
             for s in range(CAP):
-                place = got_offset[block * CAP + s]
+                place = meta[(block * CAP + s) * 2 + 1].astype(jnp.int32)
                 lanes = pl.ds(pl.multiple_of(lax.rem(place, segs) * LANES, LANES), LANES)
                 rest = place // segs
                 y, layer = lax.rem(rest, cy), rest // cy
                 tile = pl.ds(pl.multiple_of(y // 8 * 8, 8), 8)
-                misfit = got_weight[block * CAP + s] * (
+                misfit = meta[(block * CAP + s) * 2] * (
                     traj[layer, tile, lanes] - got[block, s : s + 1, :]
                 )
                 forcing[layer, tile, lanes] = forcing[layer, tile, lanes] + jnp.where(
@@ -361,7 +361,7 @@
         in_specs=edges(layers) + edges(levels) + edges(levels)
         + [whole((1, rows))] * 3 + [whole((rows, LANES))],
         out_specs=[whole(s) for s in shapes],
-        compiler_params=pltpu.CompilerParams(vmem_limit_bytes=48 << 20),
+        compiler_params=pltpu.CompilerParams(vmem_limit_bytes=60 << 20),
         name="pack",
     )(
         *[adj3] * 4, *[land_mask] * 4, *[diffusivity] * 4,
@@ -387,8 +387,7 @@
         name="exchange",
     )(*packs)
 
-    got_weight = got[:, CAP:, 0].reshape(n * CAP)
-    got_offset = got[:, CAP:, 1].reshape(n * CAP).astype(jnp.int32)
+    meta = got[:, CAP:, :2].reshape(n * CAP * 2)
     smem = pl.BlockSpec(memory_space=pltpu.SMEM)
     level3 = pl.BlockSpec((1, cy, cx), lambda i: (i, 0, 0))
     level4 = pl.BlockSpec((fields, 1, cy, cx), lambda i: (0, i, 0, 0))
@@ -396,7 +395,7 @@
         functools.partial(main_kernel, n, n_lon, n_lat, layers),
         grid=(levels,),
         out_shape=f32(*adjoint.shape),
-        in_specs=[smem, smem, smem, level4, level3, level3, whole((1, cy)),
+        in_specs=[smem, smem, level4, level3, level3, whole((1, cy)),
                   whole((layers, cy, cx)), whole(obs_shape)]
         + [whole(s) for s in came] + [whole(fold_shape)],
         out_specs=level4,
@@ -408,7 +407,7 @@
         compiler_params=pltpu.CompilerParams(vmem_limit_bytes=56 << 20),
         name="mix",
     )(
-        got_offset, got_weight, fold_partner, adjoint, diffusivity, land_mask,
+        meta, fold_partner, adjoint, diffusivity, land_mask,
         coriolis.reshape(1, cy), traj3, got, *halos, fold,
     )
 

time: 77 us -> 67.7 us (0.88)
  local copies, waits for them, and re-layouts: 11.1 us -> 1.64 us
  Pallas kernels: 63.9 us -> 65.9 us
  other arithmetic: 1.59 us -> 0 us
    unnamed x22 -> x0, local copies, waits for them, and re-layouts: 8.83 us -> none
    convert_element_type x1 -> x0, other arithmetic: 1.59 us -> none  [per_device(): got_offset = got[:, CAP:, 1].reshape(n * CAP).astype(jnp.int32)]
    pallas_call x1, Pallas kernels: 7.11 us -> 8.44 us  [per_device(): pl.pallas_call(functools.partial(pack_kernel, n, levels), grid=(1,), out_...]
where the time goes in v2:
time: 67.7 us; the launch traced here: 67.6 us
  Pallas kernels  65.9 us (97%)
  local copies, waits for them, and re-layouts  1.64 us (2%)
    pallas_call x1, Pallas kernels, per_device(): pl.pallas_call(functools.partial(main_kernel, n, n_lon, n_lat, layers), g...  38 us
    pallas_call x1, Pallas kernels, per_device(): pl.pallas_call(functools.partial(exchange_kernel, n_lon, n_lat), out_shap...  19.4 us
    pallas_call x1, Pallas kernels, per_device(): pl.pallas_call(functools.partial(pack_kernel, n, levels), grid=(1,), out_...  8.44 us

profile of v2, /device:TPU:27, one launch (start us, length us, event | category | flops | bytes accessed | tf_op | source)
XLA Modules:
  0.0 67.6 jit_solution(6926671035852399252)
XLA Ops:
  0.0 8.4 %pack.1 = (f32[3,56,512]{2,1,0:T(8,128)}, f32[3,56,512]{2,1,0:T(8,128)}, f32[64,256]{1,0:T(8,128)}, f32[64,256]{1,0:T(8,128)}, f32[32,16,128]{2,1,0:T(8,128)}) custom-call(f32[40,64,512]{2,1,0:T(8,128)} %bitcast.6, f32[40,64,512]{2,1,0:T(8,128)} %bitcast.7, f32[40,64,512]{2,1,0:T(8,128)} %bitcast.8, f32[40,64,512]{2,1,0:T(8,128)} %bitcast.9, ...), custom_call_target="tpu_custom_call" | custom-call | tf_op jit(solution)/shard_map/pack/pallas_call | solution.py:357
  8.4 19.4 %exchange.1 = (f32[3,56,512]{2,1,0:T(8,128)}, f32[3,56,512]{2,1,0:T(8,128)}, f32[64,256]{1,0:T(8,128)}, f32[64,256]{1,0:T(8,128)}, f32[8,256]{1,0:T(8,128)}, /*i...) custom-call(f32[3,56,512]{2,1,0:T(8,128)} %get-tuple-element.20.row_, ...), custom_call_target="tpu_custom_call" | custom-call | tf_op jit(solution)/shard_map/exchange/pallas_call | solution.py:375
  27.9 0.9 %slice.3 = f32[32,8,2]{2,1,0:T(8,128)S(1)} slice(f32[32,16,128]{2,1,0:T(8,128)} %get-tuple-element.25.got), slice={[0:32], [8:16], [0:2]} | slice | bytes 4096 | tf_op jit(solution)/shard_map/slice | solution.py:390
  28.8 0.7 %reshape.25.meta = f32[512]{0:T(512)} reshape(f32[32,8,2]{2,1,0:T(8,128)S(1)} %slice.3) | data formatting | bytes 4096 | tf_op jit(solution)/shard_map/reshape | solution.py:390
  29.5 38.0 %mix.1 = f32[4,10,64,512]{3,2,1,0:T(8,128)} custom-call(f32[512]{0:T(512)} %reshape.25.meta, s32[512]{0:T(512)} %partner.1, f32[4,10,64,512]{3,2,1,0:T(8,128)} %adj.1, f32[10,64,512]{2,1,0:T(8,128)} %dif.1, s32[10,64,512]{2,1,0:T(8,128)} %wet_ref.1, f32[1,64]{1,0:T(1,128)} %bitcast.11, f32[40,64,512]{2,1,0:T(8,128)} %bitcast.10, ...), custom_call_target="tpu_custom_call" | custom-call | tf_op jit(solution)/shard_map/mix/pallas_call | solution.py:394

commit v3 on v2

--- a/solution.py
+++ b/solution.py
@@ -249,16 +249,17 @@
             column = jnp.where(column < 0, column + nx, column)
             column = jnp.where(column >= nx, column - nx, column)
             within = lax.broadcasted_iota(jnp.int32, (cx, wide), 0)
+            deep = fold.shape[2]
+            total = jnp.zeros((NSUB * deep, wide), F32)
+            for t in range(n_lon):
+                pick = (within + t * cx == column).astype(F32).astype(jnp.bfloat16)
+                left = fold[t].reshape(NSUB * deep, cx)
+                for part in range(3):
+                    piece = left.astype(jnp.bfloat16)
+                    left = left - piece.astype(F32)
+                    total = total + dot(piece, pick, ((1,), (0,)), None)
             for r in range(NSUB):
-                total = jnp.zeros((fold.shape[2], wide), F32)
-                for t in range(n_lon):
-                    pick = (within + t * cx == column).astype(F32).astype(jnp.bfloat16)
-                    left = fold[t, NSUB - 1 - r]
-                    for part in range(3):
-                        piece = left.astype(jnp.bfloat16)
-                        left = left - piece.astype(F32)
-                        total = total + dot(piece, pick, ((1,), (0,)), None)
-                rim[r] = total
+                rim[r] = total[(NSUB - 1 - r) * deep : (NSUB - r) * deep]
 
     lane = lax.broadcasted_iota(jnp.int32, (cy, LANES), 1)
     lane8 = lax.broadcasted_iota(jnp.int32, (8, LANES), 1)

time: 67.7 us -> 65.3 us (0.965)
  Pallas kernels: 65.9 us -> 63.6 us
    pallas_call x1, Pallas kernels: 38 us -> 35.7 us  [per_device(): pl.pallas_call(functools.partial(main_kernel, n, n_lon, n_lat, layers), g...]
where the time goes in v3:
time: 65.3 us; the launch traced here: 65.2 us
  Pallas kernels  63.6 us (97%)
  local copies, waits for them, and re-layouts  1.64 us (3%)
    pallas_call x1, Pallas kernels, per_device(): pl.pallas_call(functools.partial(main_kernel, n, n_lon, n_lat, layers), g...  35.7 us
    pallas_call x1, Pallas kernels, per_device(): pl.pallas_call(functools.partial(exchange_kernel, n_lon, n_lat), out_shap...  19.4 us
    pallas_call x1, Pallas kernels, per_device(): pl.pallas_call(functools.partial(pack_kernel, n, levels), grid=(1,), out_...  8.44 us

profile of v3, /device:TPU:27, one launch (start us, length us, event | category | flops | bytes accessed | tf_op | source)
XLA Modules:
  0.0 65.2 jit_solution(8335763123761078927)
XLA Ops:
  0.0 8.4 %pack.1 = (f32[3,56,512]{2,1,0:T(8,128)}, f32[3,56,512]{2,1,0:T(8,128)}, f32[64,256]{1,0:T(8,128)}, f32[64,256]{1,0:T(8,128)}, f32[32,16,128]{2,1,0:T(8,128)}) custom-call(f32[40,64,512]{2,1,0:T(8,128)} %bitcast.6, f32[40,64,512]{2,1,0:T(8,128)} %bitcast.7, f32[40,64,512]{2,1,0:T(8,128)} %bitcast.8, f32[40,64,512]{2,1,0:T(8,128)} %bitcast.9, ...), custom_call_target="tpu_custom_call" | custom-call | tf_op jit(solution)/shard_map/pack/pallas_call | solution.py:358
  8.4 19.4 %exchange.1 = (f32[3,56,512]{2,1,0:T(8,128)}, f32[3,56,512]{2,1,0:T(8,128)}, f32[64,256]{1,0:T(8,128)}, f32[64,256]{1,0:T(8,128)}, f32[8,256]{1,0:T(8,128)}, /*i...) custom-call(f32[3,56,512]{2,1,0:T(8,128)} %get-tuple-element.20.row_, ...), custom_call_target="tpu_custom_call" | custom-call | tf_op jit(solution)/shard_map/exchange/pallas_call | solution.py:376
  27.9 0.9 %slice.3 = f32[32,8,2]{2,1,0:T(8,128)S(1)} slice(f32[32,16,128]{2,1,0:T(8,128)} %get-tuple-element.25.got), slice={[0:32], [8:16], [0:2]} | slice | bytes 4096 | tf_op jit(solution)/shard_map/slice | solution.py:391
  28.8 0.7 %reshape.25.meta = f32[512]{0:T(512)} reshape(f32[32,8,2]{2,1,0:T(8,128)S(1)} %slice.3) | data formatting | bytes 4096 | tf_op jit(solution)/shard_map/reshape | solution.py:391
  29.5 35.7 %mix.1 = f32[4,10,64,512]{3,2,1,0:T(8,128)} custom-call(f32[512]{0:T(512)} %reshape.25.meta, s32[512]{0:T(512)} %partner.1, f32[4,10,64,512]{3,2,1,0:T(8,128)} %adj.1, f32[10,64,512]{2,1,0:T(8,128)} %dif.1, s32[10,64,512]{2,1,0:T(8,128)} %wet_ref.1, f32[1,64]{1,0:T(1,128)} %bitcast.11, f32[40,64,512]{2,1,0:T(8,128)} %bitcast.10, ...), custom_call_target="tpu_custom_call" | custom-call | tf_op jit(solution)/shard_map/mix/pallas_call | solution.py:395
